TPU v7x, 128 devices: a whole 4x4x4 slice. The times are simulated.
128 devices in a mesh: replica: 32 (over x, y, z_lo), fsdp: 4 (over z_hi, core).
Axes of the slice: x: 4, y: 4, z: 4 (z_hi: 2, z_lo: 2; z = z_hi * 2 + z_lo), core: 2. Of those that a mesh axis runs over, the one named last changes fastest.
Arguments:
- deltas: bfloat16 [32, 2048, 5120], P('replica', 'fsdp'), may hold values from -6 to 6
- master: float32 [2048, 5120], P('fsdp', 'replica'), may hold values from -6 to 6
- momentum: float32 [2048, 5120], P('fsdp', 'replica'), may hold values from -3 to 3
- inputs: bfloat16 [32, 2048, 2560], P('replica', 'fsdp'), may hold values from -6 to 6
- inner_weight: bfloat16 [32, 2560, 2560], P('replica', 'fsdp'), may hold values from -0.125 to 0.125
- cotangent: bfloat16 [32, 2048, 2560], P('replica', 'fsdp'), may hold values from -6 to 6
Outputs:
- new_master: float32 [2048, 5120], P('fsdp', 'replica')
- new_momentum: float32 [2048, 5120], P('fsdp', 'replica')
- new_weights: bfloat16 [2048, 5120], P('fsdp')
- input_grad: bfloat16 [32, 2048, 2560], P('replica', 'fsdp')
- weight_grad: bfloat16 [32, 2560, 2560], P('replica', 'fsdp')
All inputs are finite; a program needn't handle non-finite values.
Results may differ from a plain program's by a relative error of at most 0.015.
Values may be sent and summed in bfloat16 or wider, within the bound.
A program may use at most 128 MiB of HBM per device.

v0:
```python
import jax
import jax.numpy as jnp
from jax import lax
from jax.sharding import PartitionSpec as P


def outer_step(deltas, master, momentum):
    replicas = lax.axis_size("replica")
    summed = lax.psum_scatter(
        deltas[0].astype(jnp.float32).astype(jnp.bfloat16),
        "replica",
        scatter_dimension=1,
        tiled=True,
    ).astype(jnp.float32)
    outer_grad = summed / replicas
    new_momentum = 0.9 * momentum + outer_grad
    new_master = master - 0.7 * (outer_grad + 0.9 * new_momentum)
    rounded = new_master.astype(jnp.bfloat16)
    new_weights = lax.all_gather(rounded, "replica", axis=1, tiled=True)
    return (new_master, new_momentum, new_weights)


def inner_pass(inputs, inner_weight, cotangent):
    local_in = inputs[0]
    local_co = cotangent[0]
    full_weight = lax.all_gather(inner_weight[0], "fsdp", axis=0, tiled=True)
    input_grad = lax.dot_general(
        local_co, full_weight, (((1,), (1,)), ((), ())), preferred_element_type=jnp.float32
    )
    weight_grad = lax.psum_scatter(
        lax.dot_general(
            local_in, local_co, (((0,), (0,)), ((), ())), preferred_element_type=jnp.float32
        ).astype(jnp.bfloat16),
        "fsdp",
        scatter_dimension=0,
        tiled=True,
    )
    return (input_grad.astype(jnp.bfloat16)[None], weight_grad[None])


def per_device(deltas, master, momentum, inputs, inner_weight, cotangent):
    input_grad, weight_grad = inner_pass(inputs, inner_weight, cotangent)
    new_master, new_momentum, new_weights = outer_step(deltas, master, momentum)
    return (new_master, new_momentum, new_weights, input_grad, weight_grad)


def solution(mesh):
    return jax.shard_map(
        per_device,
        mesh=mesh,
        in_specs=(
            P("replica", "fsdp", None),
            P("fsdp", "replica"),
            P("fsdp", "replica"),
            P("replica", "fsdp", None),
            P("replica", "fsdp", None),
            P("replica", "fsdp", None),
        ),
        out_specs=(
            P("fsdp", "replica"),
            P("fsdp", "replica"),
            P("fsdp", None),
            P("replica", "fsdp", None),
            P("replica", "fsdp", None),
        ),
        check_vma=False,
    )
```

profile of v0, /device:TPU:1, one launch (start us, length us, event | category | flops | bytes accessed | tf_op | source)
XLA Modules:
  0.0 540.4 jit_solution(14641560571692953485)
XLA Ops:
  8.0 0.0 copy-start
  8.0 0.0 reduce-scatter.3.cloned.1.call-start
  8.1 8.1 %copy.13 = bf16[1,512,5120]{1,2,0:T(8,128)(2,1)} copy(bf16[1,512,5120]{2,1,0:T(8,128)(2,1)} %param.6) | data formatting | bytes 10485760 | tf_op args[0]
  16.1 0.0 copy-start.1
  16.1 0.0 copy-start.2
  16.1 0.0 reduce-scatter.3.cloned.1.call-update
  16.2 0.0 all-gather.6.cloned.1.call-start
  16.2 0.5 all-gather.6.cloned.1.call-update
  16.7 0.0 all-gather.4.cloned.1.call-start
  16.8 220.3 %reduce-scatter.3.cloned.1.call-done = bf16[512,160]{0,1:T(8,128)(2,1)} async-done(((bf16[512,5120]{0,1:T(8,128)(2,1)}), bf16[512,160]{0,1:T(8,128)(2,1)}) %reduce-scatter.3.cloned.1.call-update) | async-done | bytes 163856 | tf_op jit(solution)/shard_map/reduce_scatter | solution.py:9
  237.1 0.0 copy-done.1
  237.1 0.0 copy-done.2
  237.1 1.9 fusion.11
  239.0 0.0 all-gather.4.cloned.1.call-update
  239.0 0.0 reduce-scatter.5.cloned.1.call-start
  239.1 0.0 copy-done
  239.1 11.9 %convolution_convert_fusion = bf16[2560,2560]{1,0:T(8,128)(2,1)} fusion(bf16[1,512,2560]{2,1,0:T(8,128)(2,1)} %param.9, bf16[1,512,2560]{2,1,0:T(8,128)(2,1)S(1)} %copy-done), kind=kOutput, calls=%fused_computation | convolution fusion | flops 6717440000 | bytes 18350080 | tf_op jit(solution)/shard_map/dot_general | solution.py:31
  251.0 0.0 reduce-scatter.5.cloned.1.call-update
  251.0 0.0 all-gather.6.cloned.1.call-done
  251.0 11.1 %fusion.5 = bf16[1,512,2560]{2,1,0:T(8,128)(2,1)} fusion(bf16[1,2560,2560]{2,1,0:T(8,128)(2,1)} %all-gather.6.cloned.1.call-done, bf16[1,512,2560]{2,1,0:T(8,128)(2,1)S(1)} %copy-done), kind=kOutput, calls=%fused_computation.4 | convolution fusion | flops 6712197120 | bytes 18350080 | tf_op jit(solution)/shard_map/dot_general | solution.py:27
  262.1 139.2 %all-gather.4.cloned.1.call-done = bf16[512,5120]{0,1:T(8,128)(2,1)} async-done(((bf16[512,160]{0,1:T(8,128)(2,1)}), bf16[512,5120]{0,1:T(8,128)(2,1)}) %all-gather.4.cloned.1.call-update) | async-done | bytes 5242896 | tf_op jit(solution)/shard_map/all_gather | solution.py:19
  401.3 7.9 %copy.14 = bf16[512,5120]{1,0:T(8,128)(2,1)} copy(bf16[512,5120]{0,1:T(8,128)(2,1)} %all-gather.4.cloned.1.call-done) | data formatting | bytes 10485760
  409.2 123.6 %reduce-scatter.5.cloned.1.call-done = bf16[640,2560]{1,0:T(8,128)(2,1)} async-done(((bf16[2560,2560]{1,0:T(8,128)(2,1)}), bf16[640,2560]{1,0:T(8,128)(2,1)}) %reduce-scatter.5.cloned.1.call-update) | async-done | bytes 3276816 | tf_op jit(solution)/shard_map/reduce_scatter | solution.py:30
Async XLA Ops:
  8.0 231.1 %copy-start = (bf16[1,512,2560]{2,1,0:T(8,128)(2,1)S(1)}, bf16[1,512,2560]{2,1,0:T(8,128)(2,1)}, u32[]{:S(2)}) copy-start(bf16[1,512,2560]{2,1,0:T(8,128)(2,1)} %param.11) | copy-start | bytes 7864324
  8.0 229.1 %reduce-scatter.3.cloned.1.call-start = ((), (), s32[]{:S(2)}) async-start(), calls=%async_computation.2 | async-start | bytes 5406720 | tf_op jit(solution)/shard_map/reduce_scatter | solution.py:9
  16.1 221.0 %copy-start.1 = (f32[512,160]{0,1:T(8,128)S(1)}, f32[512,160]{0,1:T(8,128)}, u32[]{:S(2)}) copy-start(f32[512,160]{0,1:T(8,128)} %param.7) | copy-start | bytes 983044
  16.1 221.0 %copy-start.2 = (f32[512,160]{0,1:T(8,128)S(1)}, f32[512,160]{0,1:T(8,128)}, u32[]{:S(2)}) copy-start(f32[512,160]{0,1:T(8,128)} %param.8) | copy-start | bytes 983044
  16.2 234.9 %all-gather.6.cloned.1.call-start = ((), (), s32[]{:S(2)}) async-start(), calls=%async_computation.5 | async-start | bytes 16384000 | tf_op jit(solution)/shard_map/all_gather | solution.py:26
  16.7 384.6 %all-gather.4.cloned.1.call-start = ((), (), s32[]{:S(2)}) async-start(), calls=%async_computation.3 | async-start | bytes 5406720 | tf_op jit(solution)/shard_map/all_gather | solution.py:19
  239.0 293.8 %reduce-scatter.5.cloned.1.call-start = ((), (), s32[]{:S(2)}) async-start(), calls=%async_computation.4 | async-start | bytes 16384000 | tf_op jit(solution)/shard_map/reduce_scatter | solution.py:30
Sparse Core Ops, SparseCore 0:
  16.3 220.7 reduce-scatter.2
Sparse Core Ops, SparseCore 1:
  18.3 97.9 all-gather.5
  239.1 162.1 all-gather.3
  404.5 128.3 reduce-scatter.4
where the time goes:
time: 541 us; the launch traced here: 540 us
  waiting for transfers between devices  484 us (89%)
  matrix products  23 us (4%)
  local copies, waits for them, and re-layouts  16 us (3%)
  between operations  15.7 us (3%)
    reduce_scatter x1, waiting for transfers between devices, outer_step(): lax.psum_scatter(deltas[0].astype(jnp.float32).astype(jnp.bfloat16), 'rep...  220 us
    all_gather x1, waiting for transfers between devices, outer_step(): new_weights = lax.all_gather(rounded, 'replica', axis=1, tiled=True)  139 us
    reduce_scatter x1, waiting for transfers between devices, inner_pass(): lax.psum_scatter(lax.dot_general(local_in, local_co, (((0,), (0,)), ((),...  124 us
    unnamed x8, local copies, waits for them, and re-layouts  16 us
    dot_general x1, matrix products, inner_pass(): lax.dot_general(local_in, local_co, (((0,), (0,)), ((), ())), preferred_e...  11.9 us
    dot_general x1, matrix products, inner_pass(): lax.dot_general(local_co, full_weight, (((1,), (1,)), ((), ())), preferre...  11.1 us
  transfers between devices with their start and end apart: 4, of which 3 were waited for; matrix products, arithmetic and copies ran while one was open for 6% of the time, Pallas kernels for 0%

commit v1 on v0

v1 whole, which is shorter than its diff:
```python
import functools

import jax
import jax.numpy as jnp
from jax import lax
from jax.experimental import pallas as pl
from jax.experimental.pallas import tpu as pltpu
from jax.sharding import PartitionSpec as P

MESH = pl.DeviceIdType.MESH
BF16 = jnp.bfloat16
F32 = jnp.float32

ROWS, D = 512, 5120
HALF = ROWS // 2
XC, YC, ZC = D // 4, D // 16, D // 32
TOK, DIN, DOUT, KC = 512, 2560, 2560, 640
FIRST, SECOND = 7, 2
REPLICAS = 32
N_SEMS = 96
N_LOCAL = 32


def ds(start, size):
    return pl.ds(pl.multiple_of(start, size), size)


def kernel(
    deltas, master, momentum, inputs, weight, cotangent,
    o_master, o_momentum, o_weights, o_input_grad, o_weight_grad,
    c_all, i_all, i_t, w_all, d_all, g_all,
    a_in, b_in, b_t, b1, a_t, v_b, a2, b2, u_f, u_b, r3,
    mast, mom, new, new_a, new_ar, new_b, new_br,
    send_sems, recv_sems, local_sems,
):
    r, f = lax.axis_index("replica"), lax.axis_index("fsdp")
    x, y, zl = r // 8, (r // 2) % 4, r % 2
    h, c = f // 2, f % 2

    def replica_at(x_at, y_at, z_at):
        return ((x_at * 4 + y_at) * 2 + z_at, f)

    over_x = [replica_at((x + j) % 4, y, zl) for j in (1, 2, 3)]
    over_y = [replica_at(x, (y + j) % 4, zl) for j in (1, 2, 3)]
    over_z = replica_at(x, y, 1 - zl)
    f_s, f_p, f_q = h * 2 + 1 - c, (1 - h) * 2 + c, (1 - h) * 2 + 1 - c
    sibling, far, diagonal = (r, f_s), (r, f_p), (r, f_q)

    counts = {"remote": 0, "local": 0}
    sent = []
    stored = []

    def remote(src, dst, device):
        i = counts["remote"]
        counts["remote"] += 1
        copy = pltpu.make_async_remote_copy(
            src_ref=src, dst_ref=dst, send_sem=send_sems.at[i], recv_sem=recv_sems.at[i],
            device_id=device, device_id_type=MESH,
        )
        copy.start()
        sent.append(copy)
        return copy

    def local(src, dst):
        i = counts["local"]
        counts["local"] += 1
        copy = pltpu.make_async_copy(src, dst, local_sems.at[i])
        copy.start()
        return copy

    def store(src, dst):
        stored.append(local(src, dst))

    barrier = pltpu.get_barrier_semaphore()
    partners = over_x + over_y + [over_z, sibling, far, diagonal]
    for device in partners:
        pl.semaphore_signal(barrier, inc=1, device_id=device, device_id_type=MESH)
    pl.semaphore_wait(barrier, len(partners))

    far_c, far_i = [], []
    queue = []
    for j in range(8):
        rows = pl.ds(64 * j, 64)
        queue.append((far_c, cotangent.at[0, rows], c_all.at[2, rows], far))
    for j in range(2):
        rows = pl.ds(256 * j, 256)
        for slot, owner, device in ((2, f_p, far), (3, f_q, diagonal)):
            queue.append((far_i, inputs.at[0, rows, ds(owner * KC, KC)], i_all.at[slot, rows], device))

    def send_far(count):
        for _ in range(count):
            kept, src, dst, device = queue.pop(0)
            kept.append(remote(src, dst, device))

    send_far(2)
    load_b = [
        local(deltas.at[0, pl.ds(HALF, HALF), pl.ds(XC * k, XC)], b_in.at[:, pl.ds(XC * k, XC)])
        for k in range(4)
    ]
    a1 = []
    for j in (1, 3, 2):
        there = (x + j) % 4
        a1.append(remote(deltas.at[0, pl.ds(0, HALF), ds(there * XC, XC)], a_in.at[j], over_x[j - 1]))
    send_far(FIRST - 2)
    load_a = local(deltas.at[0, pl.ds(0, HALF), ds(x * XC, XC)], a_in.at[0])
    load_c = local(cotangent.at[0], c_all.at[0])
    load_w = local(weight.at[0], w_all)
    load_i = local(inputs.at[0, :, ds(f * KC, KC)], i_all.at[0])
    load_m = [local(master, mast), local(momentum, mom)]

    b1_in = []
    for k in range(4):
        load_b[k].wait()

        @pl.loop(0, XC // 256)
        def _(n):
            b_t[k, ds(n * 256, 256), :] = b_in[:, ds(XC * k + n * 256, 256)].T

        for j in (1, 3, 2):
            there = (y + j) % 4
            b1_in.append(remote(b_t.at[k, ds(there * YC, YC)], b1.at[j - 1, k], over_y[j - 1]))

    near_c = remote(cotangent.at[0], c_all.at[1], sibling)
    near_i = remote(inputs.at[0, :, ds(f_s * KC, KC)], i_all.at[1], sibling)

    def grad_of(slot):
        @pl.loop(0, 2)
        def _(n):
            rows = ds(n * 256, 256)
            d_all[slot, rows, :] = lax.dot_general(
                c_all[slot, rows, :], w_all[...], (((1,), (1,)), ((), ())),
                preferred_element_type=F32,
            ).astype(BF16)

    def turn(slot):
        @pl.loop(0, KC // 128)
        def _(n):
            i_t[slot, ds(n * 128, 128), :] = i_all[slot, :, ds(n * 128, 128)].T

    mine = ds(f * KC, KC)
    load_c.wait()
    load_w.wait()
    grad_of(0)
    store(d_all.at[0], o_input_grad.at[0, :, mine])
    near_c.wait_recv()
    grad_of(1)
    grads = [remote(d_all.at[1], o_input_grad.at[0, :, mine], sibling)]
    load_i.wait()
    turn(0)
    near_i.wait_recv()
    turn(1)

    load_a.wait()
    for copy in a1:
        copy.wait_recv()

    @pl.loop(0, XC // 128)
    def _(n):
        columns = ds(n * 128, 128)
        total = a_in[0, :, columns].astype(F32)
        for j in (1, 2, 3):
            total += a_in[j, :, columns].astype(F32)
        a_t[columns, :] = total.astype(BF16).T

    a2_in = []
    for j in (1, 3, 2):
        there = (y + j) % 4
        a2_in.append(remote(a_t.at[ds(there * YC, YC)], a2.at[j - 1], over_y[j - 1]))
    for copy in b1_in:
        copy.wait_recv()

    @pl.loop(0, 4)
    def _(k):
        @pl.loop(0, YC // 64)
        def _(n):
            rows = ds(n * 64, 64)
            total = b_t[k, ds(y * YC + n * 64, 64), :].astype(F32)
            for j in range(3):
                total += b1[j, k, rows, :].astype(F32)
            v_b[k, rows, :] = total.astype(BF16)

    b2_in = []
    for j in (1, 3, 2):
        b2_in.append(remote(v_b.at[(x + j) % 4], b2.at[j - 1], over_x[j - 1]))

    for copy in a2_in + b2_in:
        copy.wait_recv()

    @pl.loop(0, YC // 32)
    def _(n):
        rows = ds(n * 32, 32)
        total_a = a_t[ds(y * YC + n * 32, 32), :].astype(F32)
        total_b = v_b[x, rows, :].astype(F32)
        for j in range(3):
            total_a += a2[j, rows, :].astype(F32)
            total_b += b2[j, rows, :].astype(F32)
        u_f[rows, pl.ds(0, HALF)] = total_a
        u_f[rows, pl.ds(HALF, HALF)] = total_b
        u_b[rows, pl.ds(0, HALF)] = total_a.astype(BF16)
        u_b[rows, pl.ds(HALF, HALF)] = total_b.astype(BF16)

    z_in = remote(u_b.at[ds((1 - zl) * ZC, ZC)], r3, over_z)
    send_far(SECOND)
    for copy in load_m:
        copy.wait()
    z_in.wait_recv()

    @pl.loop(0, ZC // 32)
    def _(n):
        rows = ds(n * 32, 32)
        outer_grad = (u_f[ds(zl * ZC + n * 32, 32), :] + r3[rows, :].astype(F32)) / REPLICAS
        new_momentum = 0.9 * mom[rows, :] + outer_grad
        new_master = mast[rows, :] - 0.7 * (outer_grad + 0.9 * new_momentum)
        mom[rows, :] = new_momentum
        mast[rows, :] = new_master
        new[ds(zl * ZC + n * 32, 32), :] = new_master.astype(BF16)

    n_in = remote(new.at[ds(zl * ZC, ZC)], new.at[ds(zl * ZC, ZC)], over_z)
    send_far(len(queue))
    store(mast, o_master)
    store(mom, o_momentum)
    n_in.wait_recv()

    second = []
    here = ds(y * YC, YC)
    for j in (1, 3, 2):
        second.append(remote(new.at[:, pl.ds(0, HALF)], new_a.at[here], over_y[j - 1]))
        second.append(remote(new.at[:, pl.ds(HALF, HALF)], new_b.at[x, here], over_x[j - 1]))

    @pl.loop(0, YC // 32)
    def _(n):
        rows = ds(n * 32, 32)
        new_a[ds(y * YC + n * 32, 32), :] = new[rows, pl.ds(0, HALF)]
        new_b[x, ds(y * YC + n * 32, 32), :] = new[rows, pl.ds(HALF, HALF)]

    forwards = []
    for j in range(4):
        for copy in far_c[2 * j : 2 * j + 2]:
            copy.wait_recv()
        rows = pl.ds(128 * j, 128)
        if j < 3:
            forwards.append(remote(c_all.at[2, rows], c_all.at[3, rows], sibling))
    for copy in second:
        copy.wait_recv()
    first = []
    for j in (1, 3, 2):
        first.append(remote(new_b.at[:, here], new_b.at[:, here], over_y[j - 1]))

    @pl.loop(0, XC // 128)
    def _(n):
        new_ar[:, ds(n * 128, 128)] = new_a[ds(n * 128, 128), :].T

    theirs = o_weights.at[pl.ds(0, HALF), ds(x * XC, XC)]
    for j in (1, 3, 2):
        first.append(remote(new_ar, theirs, over_x[j - 1]))
    store(new_ar, theirs)
    forwards.append(remote(c_all.at[2, pl.ds(384, 128)], c_all.at[3, pl.ds(384, 128)], sibling))

    grad_of(2)
    grads.append(remote(d_all.at[2], o_input_grad.at[0, :, mine], far))
    for copy in forwards:
        copy.wait_recv()
    grad_of(3)
    grads.append(remote(d_all.at[3], o_input_grad.at[0, :, mine], diagonal))

    for copy in far_i[0::2]:
        copy.wait_recv()
    turn(2)
    for copy in far_i[1::2]:
        copy.wait_recv()
    turn(3)

    @pl.loop(0, DOUT // 256)
    def _(n):
        columns = ds(n * 256, 256)
        total = jnp.dot(i_t[0], c_all[0, :, columns], preferred_element_type=F32)
        for slot in (1, 2, 3):
            total += jnp.dot(i_t[slot], c_all[slot, :, columns], preferred_element_type=F32)
        g_all[:, columns] = total.astype(BF16)

    store(g_all, o_weight_grad.at[0])

    for copy in first:
        copy.wait_recv()
    for k in range(4):
        @pl.loop(0, XC // 256)
        def _(n):
            new_br[:, ds(XC * k + n * 256, 256)] = new_b[k, ds(n * 256, 256), :].T

        columns = pl.ds(XC * k, XC)
        store(new_br.at[:, columns], o_weights.at[pl.ds(HALF, HALF), columns])

    for copy in grads:
        copy.wait_recv()
    for copy in sent:
        copy.wait_send()
    for copy in stored:
        copy.wait()


def per_device(deltas, master, momentum, inputs, inner_weight, cotangent):
    shape = jax.ShapeDtypeStruct
    anywhere = pl.BlockSpec(memory_space=pl.ANY)
    vmem = pltpu.VMEM
    outs = pl.pallas_call(
        kernel,
        out_shape=(
            shape((ZC, ROWS), F32),
            shape((ZC, ROWS), F32),
            shape((ROWS, D), BF16),
            shape((1, TOK, DIN), BF16),
            shape((1, KC, DOUT), BF16),
        ),
        in_specs=[anywhere] * 6,
        out_specs=(anywhere,) * 5,
        scratch_shapes=[
            vmem((4, TOK, DOUT), BF16),
            vmem((4, TOK, KC), BF16),
            vmem((4, KC, TOK), BF16),
            vmem((KC, DOUT), BF16),
            vmem((4, TOK, KC), BF16),
            vmem((KC, DOUT), BF16),
            vmem((4, HALF, XC), BF16),
            vmem((HALF, D), BF16),
            vmem((4, XC, HALF), BF16),
            vmem((3, 4, YC, HALF), BF16),
            vmem((XC, HALF), BF16),
            vmem((4, YC, HALF), BF16),
            vmem((3, YC, HALF), BF16),
            vmem((3, YC, HALF), BF16),
            vmem((YC, ROWS), F32),
            vmem((YC, ROWS), BF16),
            vmem((ZC, ROWS), BF16),
            vmem((ZC, ROWS), F32),
            vmem((ZC, ROWS), F32),
            vmem((YC, ROWS), BF16),
            vmem((XC, HALF), BF16),
            vmem((HALF, XC), BF16),
            vmem((4, XC, HALF), BF16),
            vmem((HALF, D), BF16),
            pltpu.SemaphoreType.DMA((N_SEMS,)),
            pltpu.SemaphoreType.DMA((N_SEMS,)),
            pltpu.SemaphoreType.DMA((N_LOCAL,)),
        ],
        compiler_params=pltpu.CompilerParams(
            collective_id=0, has_side_effects=True, vmem_limit_bytes=60 * 1024 * 1024
        ),
        cost_estimate=pl.CostEstimate(
            flops=4 * TOK * DIN * DOUT, bytes_accessed=40 * 1024 * 1024, transcendentals=0
        ),
        name="outer_step_and_projection_grads",
    )(deltas, master.T, momentum.T, inputs, inner_weight, cotangent)
    new_master, new_momentum, new_weights, input_grad, weight_grad = outs
    return (new_master.T, new_momentum.T, new_weights, input_grad, weight_grad)


def solution(mesh):
    return jax.shard_map(
        per_device,
        mesh=mesh,
        in_specs=(
            P("replica", "fsdp", None),
            P("fsdp", "replica"),
            P("fsdp", "replica"),
            P("replica", "fsdp", None),
            P("replica", "fsdp", None),
            P("replica", "fsdp", None),
        ),
        out_specs=(
            P("fsdp", "replica"),
            P("fsdp", "replica"),
            P("fsdp", None),
            P("replica", "fsdp", None),
            P("replica", "fsdp", None),
        ),
        check_vma=False,
    )
```

time: 541 us -> 144 us (0.27)
  waiting for transfers between devices: 484 us -> 0 us
  Pallas kernels: 0 us -> 130 us
  matrix products: 23 us -> 0 us
  between operations: 15.7 us -> 0.65 us
    reduce_scatter x2 -> x0, waiting for transfers between devices: 344 us -> none  [the longest x1 220 us: outer_step(): lax.psum_scatter(deltas[0].astype(jnp.float32).astype(jnp.bfloat16), 'rep...]
    all_gather x2 -> x0, waiting for transfers between devices: 139 us -> none  [the longest x1 139 us: outer_step(): new_weights = lax.all_gather(rounded, 'replica', axis=1, tiled=True)]
    pallas_call x0 -> x1, Pallas kernels: none -> 130 us  [per_device(): pl.pallas_call(kernel, out_shape=(shape((ZC, ROWS), F32), shape((ZC, ROWS...]
    dot_general x2 -> x0, matrix products: 23 us -> none  [the longest x1 11.9 us: inner_pass(): lax.dot_general(local_in, local_co, (((0,), (0,)), ((), ())), preferred_e...]
    unnamed x8 -> x9, local copies, waits for them, and re-layouts: 16 us -> 13.3 us
  transfers between devices with their start and end apart: 4 -> 0, of which waited for: 3 -> 0; matrix products, arithmetic and copies ran while one was open for 6% -> 0% of each run, Pallas kernels for 0% -> 0%
where the time goes in v1:
time: 144 us
  Pallas kernels  130 us (90%)
  local copies, waits for them, and re-layouts  13.3 us (9%)
    pallas_call x1, Pallas kernels, per_device(): pl.pallas_call(kernel, out_shape=(shape((ZC, ROWS), F32), shape((ZC, ROWS...  130 us
    unnamed x9, local copies, waits for them, and re-layouts  13.3 us

profile of v1, /device:TPU:1, one launch (start us, length us, event | category | flops | bytes accessed | tf_op | source)
XLA Modules:
  0.0 144.2 jit_solution(3742421706099078593)
XLA Ops:
  0.6 130.2 %outer_step_and_projection_grads.1 = (f32[160,512]{1,0:T(8,128)}, f32[160,512]{1,0:T(8,128)}, bf16[512,5120]{1,0:T(8,128)(2,1)}, bf16[1,512,2560]{2,1,0:T(8,128)(2,1)}, bf16[1,640,2560]{2,1,0:T(8,128)(2,1)}) custom-call(bf16[1,512,5120]{2,1,0:T(8,128)(2,1)} %deltas.1, f32[160,512]{1,0:T(8,128)} %bitcast.6, f32[160,512]{1,0:T(8,128)} %bitcast.7, ...), custom_call_target="tpu_custom_call" | custom-call | flops 13421772800 | bytes 41943040 | tf_op jit(solution)/shard_map/outer_step_and_projection_grads/pallas_call | solution.py:305
  130.9 1.7 %copy.16 = f32[512,160]{0,1:T(8,128)} copy(f32[512,160]{0,1:T(8,128)} %bitcast.5) | data formatting | bytes 655360
  132.6 1.7 %copy.17 = f32[512,160]{0,1:T(8,128)} copy(f32[512,160]{0,1:T(8,128)} %bitcast.4) | data formatting | bytes 655360
  134.3 0.0 copy-start.1
  134.3 5.3 %copy.18 = bf16[512,5120]{1,0:T(8,128)(2,1)} copy(bf16[512,5120]{1,0:T(8,128)(2,1)} %get-tuple-element.22) | data formatting | bytes 10485760
  139.7 0.0 copy-done.1
  139.7 0.0 copy-start
  139.7 1.5 %copy.19 = bf16[1,512,2560]{2,1,0:T(8,128)(2,1)} copy(bf16[1,512,2560]{2,1,0:T(8,128)(2,1)S(1)} %copy-done.1) | data formatting | bytes 5242880
  141.2 1.4 copy-done
  142.5 1.7 %copy.20 = bf16[1,640,2560]{2,1,0:T(8,128)(2,1)} copy(bf16[1,640,2560]{2,1,0:T(8,128)(2,1)S(1)} %copy-done) | data formatting | bytes 6553600
Async XLA Ops:
  134.3 5.3 %copy-start.1 = (bf16[1,512,2560]{2,1,0:T(8,128)(2,1)S(1)}, bf16[1,512,2560]{2,1,0:T(8,128)(2,1)}, u32[]{:S(2)}) copy-start(bf16[1,512,2560]{2,1,0:T(8,128)(2,1)} %get-tuple-element.23) | copy-start | bytes 7864324
  139.7 2.9 %copy-start = (bf16[1,640,2560]{2,1,0:T(8,128)(2,1)S(1)}, bf16[1,640,2560]{2,1,0:T(8,128)(2,1)}, u32[]{:S(2)}) copy-start(bf16[1,640,2560]{2,1,0:T(8,128)(2,1)} %get-tuple-element.24) | copy-start | bytes 9830404

commit v2 on v1

--- a/solution.py
+++ b/solution.py
@@ -15,7 +15,7 @@
 HALF = ROWS // 2
 XC, YC, ZC = D // 4, D // 16, D // 32
 TOK, DIN, DOUT, KC = 512, 2560, 2560, 640
-FIRST, SECOND = 7, 2
+FIRST, SECOND = 1, 2
 REPLICAS = 32
 N_SEMS = 96
 N_LOCAL = 32
@@ -30,7 +30,7 @@
     o_master, o_momentum, o_weights, o_input_grad, o_weight_grad,
     c_all, i_all, i_t, w_all, d_all, g_all,
     a_in, b_in, b_t, b1, a_t, v_b, a2, b2, u_f, u_b, r3,
-    mast, mom, new, new_a, new_ar, new_b, new_br,
+    mast, mom, new, new_a, new_ar, new_b,
     send_sems, recv_sems, local_sems,
 ):
     r, f = lax.axis_index("replica"), lax.axis_index("fsdp")
@@ -79,11 +79,11 @@
 
     far_c, far_i = [], []
     queue = []
-    for j in range(8):
-        rows = pl.ds(64 * j, 64)
+    for start, size in ((0, 448), (448, 64)):
+        rows = pl.ds(start, size)
         queue.append((far_c, cotangent.at[0, rows], c_all.at[2, rows], far))
-    for j in range(2):
-        rows = pl.ds(256 * j, 256)
+    for start, size in ((0, 256), (256, 256)):
+        rows = pl.ds(start, size)
         for slot, owner, device in ((2, f_p, far), (3, f_q, diagonal)):
             queue.append((far_i, inputs.at[0, rows, ds(owner * KC, KC)], i_all.at[slot, rows], device))
 
@@ -92,7 +92,7 @@
             kept, src, dst, device = queue.pop(0)
             kept.append(remote(src, dst, device))
 
-    send_far(2)
+    send_far(FIRST)
     load_b = [
         local(deltas.at[0, pl.ds(HALF, HALF), pl.ds(XC * k, XC)], b_in.at[:, pl.ds(XC * k, XC)])
         for k in range(4)
@@ -101,7 +101,6 @@
     for j in (1, 3, 2):
         there = (x + j) % 4
         a1.append(remote(deltas.at[0, pl.ds(0, HALF), ds(there * XC, XC)], a_in.at[j], over_x[j - 1]))
-    send_far(FIRST - 2)
     load_a = local(deltas.at[0, pl.ds(0, HALF), ds(x * XC, XC)], a_in.at[0])
     load_c = local(cotangent.at[0], c_all.at[0])
     load_w = local(weight.at[0], w_all)
@@ -234,12 +233,9 @@
         new_b[x, ds(y * YC + n * 32, 32), :] = new[rows, pl.ds(HALF, HALF)]
 
     forwards = []
-    for j in range(4):
-        for copy in far_c[2 * j : 2 * j + 2]:
-            copy.wait_recv()
-        rows = pl.ds(128 * j, 128)
-        if j < 3:
-            forwards.append(remote(c_all.at[2, rows], c_all.at[3, rows], sibling))
+    for copy, rows in zip(far_c, (pl.ds(0, 448), pl.ds(448, 64))):
+        copy.wait_recv()
+        forwards.append(remote(c_all.at[2, rows], c_all.at[3, rows], sibling))
     for copy in second:
         copy.wait_recv()
     first = []
@@ -254,7 +250,6 @@
     for j in (1, 3, 2):
         first.append(remote(new_ar, theirs, over_x[j - 1]))
     store(new_ar, theirs)
-    forwards.append(remote(c_all.at[2, pl.ds(384, 128)], c_all.at[3, pl.ds(384, 128)], sibling))
 
     grad_of(2)
     grads.append(remote(d_all.at[2], o_input_grad.at[0, :, mine], far))
@@ -285,10 +280,10 @@
     for k in range(4):
         @pl.loop(0, XC // 256)
         def _(n):
-            new_br[:, ds(XC * k + n * 256, 256)] = new_b[k, ds(n * 256, 256), :].T
+            b_in[:, ds(XC * k + n * 256, 256)] = new_b[k, ds(n * 256, 256), :].T
 
         columns = pl.ds(XC * k, XC)
-        store(new_br.at[:, columns], o_weights.at[pl.ds(HALF, HALF), columns])
+        store(b_in.at[:, columns], o_weights.at[pl.ds(HALF, HALF), columns])
 
     for copy in grads:
         copy.wait_recv()
@@ -298,18 +293,25 @@
         copy.wait()
 
 
+def hand_over(*refs):
+    copies = [pltpu.make_async_copy(refs[i], refs[5 + i], refs[10].at[i]) for i in (2, 4, 3, 0, 1)]
+    for copy in copies:
+        copy.start()
+    for copy in copies:
+        copy.wait()
+
+
 def per_device(deltas, master, momentum, inputs, inner_weight, cotangent):
-    shape = jax.ShapeDtypeStruct
     anywhere = pl.BlockSpec(memory_space=pl.ANY)
     vmem = pltpu.VMEM
     outs = pl.pallas_call(
         kernel,
         out_shape=(
-            shape((ZC, ROWS), F32),
-            shape((ZC, ROWS), F32),
-            shape((ROWS, D), BF16),
-            shape((1, TOK, DIN), BF16),
-            shape((1, KC, DOUT), BF16),
+            vmem((ZC, ROWS), F32),
+            vmem((ZC, ROWS), F32),
+            vmem((ROWS, D), BF16),
+            vmem((1, TOK, DIN), BF16),
+            vmem((1, KC, DOUT), BF16),
         ),
         in_specs=[anywhere] * 6,
         out_specs=(anywhere,) * 5,
@@ -337,20 +339,27 @@
             vmem((XC, HALF), BF16),
             vmem((HALF, XC), BF16),
             vmem((4, XC, HALF), BF16),
-            vmem((HALF, D), BF16),
             pltpu.SemaphoreType.DMA((N_SEMS,)),
             pltpu.SemaphoreType.DMA((N_SEMS,)),
             pltpu.SemaphoreType.DMA((N_LOCAL,)),
         ],
         compiler_params=pltpu.CompilerParams(
-            collective_id=0, has_side_effects=True, vmem_limit_bytes=60 * 1024 * 1024
+            collective_id=0, has_side_effects=True, vmem_limit_bytes=46 * 1024 * 1024
         ),
         cost_estimate=pl.CostEstimate(
             flops=4 * TOK * DIN * DOUT, bytes_accessed=40 * 1024 * 1024, transcendentals=0
         ),
         name="outer_step_and_projection_grads",
     )(deltas, master.T, momentum.T, inputs, inner_weight, cotangent)
-    new_master, new_momentum, new_weights, input_grad, weight_grad = outs
+    new_master, new_momentum, new_weights, input_grad, weight_grad = pl.pallas_call(
+        hand_over,
+        out_shape=tuple(jax.ShapeDtypeStruct(out.shape, out.dtype) for out in outs),
+        in_specs=[anywhere] * 5,
+        out_specs=(anywhere,) * 5,
+        scratch_shapes=[pltpu.SemaphoreType.DMA((5,))],
+        compiler_params=pltpu.CompilerParams(vmem_limit_bytes=1024 * 1024),
+        name="hand_over",
+    )(*(pltpu.with_memory_space_constraint(out, pltpu.VMEM) for out in outs))
     return (new_master.T, new_momentum.T, new_weights, input_grad, weight_grad)
 
 

time: 144 us -> 135 us (0.938)
  local copies, waits for them, and re-layouts: 13.3 us -> 0 us
  Pallas kernels: 130 us -> 134 us
    unnamed x9 -> x0, local copies, waits for them, and re-layouts: 13.3 us -> none
    pallas_call x1 -> x2, Pallas kernels: 130 us -> 134 us  [the longest x1 130 us: per_device(): pl.pallas_call(kernel, out_shape=(vmem((ZC, ROWS), F32), vmem((ZC, ROWS),...]
where the time goes in v2:
time: 135 us
  Pallas kernels  134 us (99%)
    pallas_call x1, Pallas kernels, per_device(): pl.pallas_call(kernel, out_shape=(vmem((ZC, ROWS), F32), vmem((ZC, ROWS),...  130 us
    pallas_call x1, Pallas kernels, per_device(): pl.pallas_call(hand_over, out_shape=tuple((jax.ShapeDtypeStruct(out.shape...  4.37 us

profile of v2, /device:TPU:1, one launch (start us, length us, event | category | flops | bytes accessed | tf_op | source)
XLA Modules:
  0.0 135.1 jit_solution(882111903746443961)
XLA Ops:
  0.6 130.1 %outer_step_and_projection_grads.1 = (f32[160,512]{1,0:T(8,128)S(1)}, f32[160,512]{1,0:T(8,128)S(1)}, bf16[512,5120]{1,0:T(8,128)(2,1)S(1)}, bf16[1,512,2560]{2,1,0:T(8,128)(2,1)S(1)}, bf16[1,640,2560]{2,1,0:T(8,128)(2,1)S(1)}) custom-call(bf16[1,512,5120]{2,1,0:T(8,128)(2,1)} %deltas.1, f32[160,512]{1,0:T(8,128)} %bitcast.4, f32[160,512]{1,0:T(8,128)} %bitcast.5, ...), custom_call_target="tpu_custom_call" | custom-call | flops 13421772800 | bytes 41943040 | tf_op jit(solution)/shard_map/outer_step_and_projection_grads/pallas_call | solution.py:307
  130.8 4.4 %hand_over.1 = (f32[160,512]{1,0:T(8,128)}, f32[160,512]{1,0:T(8,128)}, bf16[512,5120]{1,0:T(8,128)(2,1)}, bf16[1,512,2560]{2,1,0:T(8,128)(2,1)}, bf16[1,640,2560]{2,1,0:T(8,128)(2,1)}) custom-call(f32[160,512]{1,0:T(8,128)S(1)} %get-tuple-element.15.refs_0_, f32[160,512]{1,0:T(8,128)S(1)} %get-tuple-element.16.refs_1_, ...), custom_call_target="tpu_custom_call" | custom-call | tf_op jit(solution)/shard_map/hand_over/pallas_call | solution.py:354

commit v3 on v2

--- a/solution.py
+++ b/solution.py
@@ -15,7 +15,7 @@
 HALF = ROWS // 2
 XC, YC, ZC = D // 4, D // 16, D // 32
 TOK, DIN, DOUT, KC = 512, 2560, 2560, 640
-FIRST, SECOND = 1, 2
+FIRST, SECOND = 1, 1
 REPLICAS = 32
 N_SEMS = 96
 N_LOCAL = 32
@@ -31,7 +31,7 @@
     c_all, i_all, i_t, w_all, d_all, g_all,
     a_in, b_in, b_t, b1, a_t, v_b, a2, b2, u_f, u_b, r3,
     mast, mom, new, new_a, new_ar, new_b,
-    send_sems, recv_sems, local_sems,
+    send_sems, recv_sems, local_sems, far_sem, chip_sem, others_sem,
 ):
     r, f = lax.axis_index("replica"), lax.axis_index("fsdp")
     x, y, zl = r // 8, (r // 2) % 4, r % 2
@@ -72,10 +72,20 @@
         stored.append(local(src, dst))
 
     barrier = pltpu.get_barrier_semaphore()
-    partners = over_x + over_y + [over_z, sibling, far, diagonal]
-    for device in partners:
-        pl.semaphore_signal(barrier, inc=1, device_id=device, device_id_type=MESH)
-    pl.semaphore_wait(barrier, len(partners))
+
+    def tell(sem, device):
+        pl.semaphore_signal(sem, inc=1, device_id=device, device_id_type=MESH)
+
+    @pl.when(c == 0)
+    def _():
+        tell(barrier, far)
+        pl.semaphore_wait(barrier, 2)
+        tell(far_sem, far)
+
+    @pl.when(c == 1)
+    def _():
+        tell(barrier, sibling)
+        pl.semaphore_wait(chip_sem, 1)
 
     far_c, far_i = [], []
     queue = []
@@ -93,10 +103,28 @@
             kept.append(remote(src, dst, device))
 
     send_far(FIRST)
+
+    @pl.when(c == 0)
+    def _():
+        pl.semaphore_wait(far_sem, 1)
+        tell(chip_sem, sibling)
+
     load_b = [
         local(deltas.at[0, pl.ds(HALF, HALF), pl.ds(XC * k, XC)], b_in.at[:, pl.ds(XC * k, XC)])
         for k in range(4)
     ]
+    @pl.when(c == 1)
+    def _():
+        others = over_x + over_y + [over_z]
+        for device in others:
+            tell(barrier, device)
+        pl.semaphore_wait(barrier, len(others))
+        tell(others_sem, sibling)
+
+    @pl.when(c == 0)
+    def _():
+        pl.semaphore_wait(others_sem, 1)
+
     a1 = []
     for j in (1, 3, 2):
         there = (x + j) % 4
@@ -285,12 +313,14 @@
         columns = pl.ds(XC * k, XC)
         store(b_in.at[:, columns], o_weights.at[pl.ds(HALF, HALF), columns])
 
-    for copy in grads:
-        copy.wait_recv()
-    for copy in sent:
+    for copy in sent[:-2]:
         copy.wait_send()
     for copy in stored:
         copy.wait()
+    for copy in grads:
+        copy.wait_recv()
+    for copy in sent[-2:]:
+        copy.wait_send()
 
 
 def hand_over(*refs):
@@ -342,6 +372,9 @@
             pltpu.SemaphoreType.DMA((N_SEMS,)),
             pltpu.SemaphoreType.DMA((N_SEMS,)),
             pltpu.SemaphoreType.DMA((N_LOCAL,)),
+            pltpu.SemaphoreType.REGULAR,
+            pltpu.SemaphoreType.REGULAR,
+            pltpu.SemaphoreType.REGULAR,
         ],
         compiler_params=pltpu.CompilerParams(
             collective_id=0, has_side_effects=True, vmem_limit_bytes=46 * 1024 * 1024

time: 135 us -> 133 us (0.985)
    pallas_call x1, Pallas kernels: 130 us -> 128 us  [per_device(): pl.pallas_call(kernel, out_shape=(vmem((ZC, ROWS), F32), vmem((ZC, ROWS),...]
where the time goes in v3:
time: 133 us
  Pallas kernels  133 us (100%)
    pallas_call x1, Pallas kernels, per_device(): pl.pallas_call(kernel, out_shape=(vmem((ZC, ROWS), F32), vmem((ZC, ROWS),...  128 us
    pallas_call x1, Pallas kernels, per_device(): pl.pallas_call(hand_over, out_shape=tuple((jax.ShapeDtypeStruct(out.shape...  4.37 us

profile of v3, /device:TPU:1, one launch (start us, length us, event | category | flops | bytes accessed | tf_op | source)
XLA Modules:
  0.0 133.2 jit_solution(6182445136886966782)
XLA Ops:
  0.6 128.2 %outer_step_and_projection_grads.1 = (f32[160,512]{1,0:T(8,128)S(1)}, f32[160,512]{1,0:T(8,128)S(1)}, bf16[512,5120]{1,0:T(8,128)(2,1)S(1)}, bf16[1,512,2560]{2,1,0:T(8,128)(2,1)S(1)}, bf16[1,640,2560]{2,1,0:T(8,128)(2,1)S(1)}) custom-call(bf16[1,512,5120]{2,1,0:T(8,128)(2,1)} %deltas.1, f32[160,512]{1,0:T(8,128)} %bitcast.4, f32[160,512]{1,0:T(8,128)} %bitcast.5, ...), custom_call_target="tpu_custom_call" | custom-call | flops 13421772800 | bytes 41943040 | tf_op jit(solution)/shard_map/outer_step_and_projection_grads/pallas_call | solution.py:337
  128.9 4.4 %hand_over.1 = (f32[160,512]{1,0:T(8,128)}, f32[160,512]{1,0:T(8,128)}, bf16[512,5120]{1,0:T(8,128)(2,1)}, bf16[1,512,2560]{2,1,0:T(8,128)(2,1)}, bf16[1,640,2560]{2,1,0:T(8,128)(2,1)}) custom-call(f32[160,512]{1,0:T(8,128)S(1)} %get-tuple-element.15.refs_0_, f32[160,512]{1,0:T(8,128)S(1)} %get-tuple-element.16.refs_1_, ...), custom_call_target="tpu_custom_call" | custom-call | tf_op jit(solution)/shard_map/hand_over/pallas_call | solution.py:387

commit v4 on v3

--- a/solution.py
+++ b/solution.py
@@ -15,7 +15,7 @@
 HALF = ROWS // 2
 XC, YC, ZC = D // 4, D // 16, D // 32
 TOK, DIN, DOUT, KC = 512, 2560, 2560, 640
-FIRST, SECOND = 1, 1
+FIRST, SECOND = 1, 2
 REPLICAS = 32
 N_SEMS = 96
 N_LOCAL = 32
@@ -89,7 +89,7 @@
 
     far_c, far_i = [], []
     queue = []
-    for start, size in ((0, 448), (448, 64)):
+    for start, size in ((0, 480), (480, 32)):
         rows = pl.ds(start, size)
         queue.append((far_c, cotangent.at[0, rows], c_all.at[2, rows], far))
     for start, size in ((0, 256), (256, 256)):
@@ -261,7 +261,7 @@
         new_b[x, ds(y * YC + n * 32, 32), :] = new[rows, pl.ds(HALF, HALF)]
 
     forwards = []
-    for copy, rows in zip(far_c, (pl.ds(0, 448), pl.ds(448, 64))):
+    for copy, rows in zip(far_c, (pl.ds(0, 480), pl.ds(480, 32))):
         copy.wait_recv()
         forwards.append(remote(c_all.at[2, rows], c_all.at[3, rows], sibling))
     for copy in second:

time: 133 us -> 133 us (level)
  no operation moved by 1% of the time
where the time goes in v4:
time: 133 us
  Pallas kernels  132 us (99%)
    pallas_call x1, Pallas kernels, per_device(): pl.pallas_call(kernel, out_shape=(vmem((ZC, ROWS), F32), vmem((ZC, ROWS),...  128 us
    pallas_call x1, Pallas kernels, per_device(): pl.pallas_call(hand_over, out_shape=tuple((jax.ShapeDtypeStruct(out.shape...  4.37 us

profile of v4, /device:TPU:1, one launch (start us, length us, event | category | flops | bytes accessed | tf_op | source)
XLA Modules:
  0.0 132.5 jit_solution(11121360265510508233)
XLA Ops:
  0.6 127.5 %outer_step_and_projection_grads.1 = (f32[160,512]{1,0:T(8,128)S(1)}, f32[160,512]{1,0:T(8,128)S(1)}, bf16[512,5120]{1,0:T(8,128)(2,1)S(1)}, bf16[1,512,2560]{2,1,0:T(8,128)(2,1)S(1)}, bf16[1,640,2560]{2,1,0:T(8,128)(2,1)S(1)}) custom-call(bf16[1,512,5120]{2,1,0:T(8,128)(2,1)} %deltas.1, f32[160,512]{1,0:T(8,128)} %bitcast.4, f32[160,512]{1,0:T(8,128)} %bitcast.5, ...), custom_call_target="tpu_custom_call" | custom-call | flops 13421772800 | bytes 41943040 | tf_op jit(solution)/shard_map/outer_step_and_projection_grads/pallas_call | solution.py:337
  128.2 4.4 %hand_over.1 = (f32[160,512]{1,0:T(8,128)}, f32[160,512]{1,0:T(8,128)}, bf16[512,5120]{1,0:T(8,128)(2,1)}, bf16[1,512,2560]{2,1,0:T(8,128)(2,1)}, bf16[1,640,2560]{2,1,0:T(8,128)(2,1)}) custom-call(f32[160,512]{1,0:T(8,128)S(1)} %get-tuple-element.15.refs_0_, f32[160,512]{1,0:T(8,128)S(1)} %get-tuple-element.16.refs_1_, ...), custom_call_target="tpu_custom_call" | custom-call | tf_op jit(solution)/shard_map/hand_over/pallas_call | solution.py:387

commit v5 on v4

--- a/solution.py
+++ b/solution.py
@@ -17,8 +17,8 @@
 TOK, DIN, DOUT, KC = 512, 2560, 2560, 640
 FIRST, SECOND = 1, 2
 REPLICAS = 32
-N_SEMS = 96
-N_LOCAL = 32
+N_SEMS = 31
+N_LOCAL = 10
 
 
 def ds(start, size):
@@ -49,6 +49,7 @@
     counts = {"remote": 0, "local": 0}
     sent = []
     stored = []
+    free = []
 
     def remote(src, dst, device):
         i = counts["remote"]
@@ -61,15 +62,32 @@
         sent.append(copy)
         return copy
 
+    def together(whole, pieces):
+        i = counts["remote"]
+        counts["remote"] += 1
+        sems = {"send_sem": send_sems.at[i], "recv_sem": recv_sems.at[i], "device_id_type": MESH}
+        for src, dst, device in pieces:
+            pltpu.make_async_remote_copy(src_ref=src, dst_ref=dst, device_id=device, **sems).start()
+        copy = pltpu.make_async_remote_copy(src_ref=whole, dst_ref=whole, device_id=sibling, **sems)
+        sent.append(copy)
+        return copy
+
     def local(src, dst):
-        i = counts["local"]
-        counts["local"] += 1
+        if free:
+            i = free.pop()
+        else:
+            i = counts["local"]
+            counts["local"] += 1
         copy = pltpu.make_async_copy(src, dst, local_sems.at[i])
         copy.start()
-        return copy
+        return copy, i
+
+    def landed(load):
+        load[0].wait()
+        free.append(load[1])
 
     def store(src, dst):
-        stored.append(local(src, dst))
+        stored.append(local(src, dst)[0])
 
     barrier = pltpu.get_barrier_semaphore()
 
@@ -125,19 +143,19 @@
     def _():
         pl.semaphore_wait(others_sem, 1)
 
-    a1 = []
-    for j in (1, 3, 2):
-        there = (x + j) % 4
-        a1.append(remote(deltas.at[0, pl.ds(0, HALF), ds(there * XC, XC)], a_in.at[j], over_x[j - 1]))
+    a1_in = together(a_in.at[pl.ds(1, 3)], [
+        (deltas.at[0, pl.ds(0, HALF), ds((x + j) % 4 * XC, XC)], a_in.at[j], over_x[j - 1])
+        for j in (1, 3, 2)
+    ])
     load_a = local(deltas.at[0, pl.ds(0, HALF), ds(x * XC, XC)], a_in.at[0])
     load_c = local(cotangent.at[0], c_all.at[0])
     load_w = local(weight.at[0], w_all)
     load_i = local(inputs.at[0, :, ds(f * KC, KC)], i_all.at[0])
     load_m = [local(master, mast), local(momentum, mom)]
 
-    b1_in = []
+    b1_sems = {"send_sem": send_sems.at[counts["remote"]], "recv_sem": recv_sems.at[counts["remote"]]}
     for k in range(4):
-        load_b[k].wait()
+        landed(load_b[k])
 
         @pl.loop(0, XC // 256)
         def _(n):
@@ -145,7 +163,11 @@
 
         for j in (1, 3, 2):
             there = (y + j) % 4
-            b1_in.append(remote(b_t.at[k, ds(there * YC, YC)], b1.at[j - 1, k], over_y[j - 1]))
+            pltpu.make_async_remote_copy(
+                src_ref=b_t.at[k, ds(there * YC, YC)], dst_ref=b1.at[j - 1, k],
+                device_id=over_y[j - 1], device_id_type=MESH, **b1_sems,
+            ).start()
+    b1_in = together(b1, [])
 
     near_c = remote(cotangent.at[0], c_all.at[1], sibling)
     near_i = remote(inputs.at[0, :, ds(f_s * KC, KC)], i_all.at[1], sibling)
@@ -165,21 +187,20 @@
             i_t[slot, ds(n * 128, 128), :] = i_all[slot, :, ds(n * 128, 128)].T
 
     mine = ds(f * KC, KC)
-    load_c.wait()
-    load_w.wait()
+    landed(load_c)
+    landed(load_w)
     grad_of(0)
     store(d_all.at[0], o_input_grad.at[0, :, mine])
     near_c.wait_recv()
     grad_of(1)
     grads = [remote(d_all.at[1], o_input_grad.at[0, :, mine], sibling)]
-    load_i.wait()
+    landed(load_i)
     turn(0)
     near_i.wait_recv()
     turn(1)
 
-    load_a.wait()
-    for copy in a1:
-        copy.wait_recv()
+    landed(load_a)
+    a1_in.wait_recv()
 
     @pl.loop(0, XC // 128)
     def _(n):
@@ -189,12 +210,10 @@
             total += a_in[j, :, columns].astype(F32)
         a_t[columns, :] = total.astype(BF16).T
 
-    a2_in = []
-    for j in (1, 3, 2):
-        there = (y + j) % 4
-        a2_in.append(remote(a_t.at[ds(there * YC, YC)], a2.at[j - 1], over_y[j - 1]))
-    for copy in b1_in:
-        copy.wait_recv()
+    a2_in = together(a2, [
+        (a_t.at[ds((y + j) % 4 * YC, YC)], a2.at[j - 1], over_y[j - 1]) for j in (1, 3, 2)
+    ])
+    b1_in.wait_recv()
 
     @pl.loop(0, 4)
     def _(k):
@@ -206,12 +225,10 @@
                 total += b1[j, k, rows, :].astype(F32)
             v_b[k, rows, :] = total.astype(BF16)
 
-    b2_in = []
-    for j in (1, 3, 2):
-        b2_in.append(remote(v_b.at[(x + j) % 4], b2.at[j - 1], over_x[j - 1]))
-
-    for copy in a2_in + b2_in:
-        copy.wait_recv()
+    b2_in = together(b2, [(v_b.at[(x + j) % 4], b2.at[j - 1], over_x[j - 1]) for j in (1, 3, 2)])
+
+    a2_in.wait_recv()
+    b2_in.wait_recv()
 
     @pl.loop(0, YC // 32)
     def _(n):
@@ -228,8 +245,8 @@
 
     z_in = remote(u_b.at[ds((1 - zl) * ZC, ZC)], r3, over_z)
     send_far(SECOND)
-    for copy in load_m:
-        copy.wait()
+    for load in load_m:
+        landed(load)
     z_in.wait_recv()
 
     @pl.loop(0, ZC // 32)

time: 133 us -> 131 us (0.985)
    pallas_call x1, Pallas kernels: 128 us -> 126 us  [per_device(): pl.pallas_call(kernel, out_shape=(vmem((ZC, ROWS), F32), vmem((ZC, ROWS),...]
where the time goes in v5:
time: 131 us
  Pallas kernels  131 us (100%)
    pallas_call x1, Pallas kernels, per_device(): pl.pallas_call(kernel, out_shape=(vmem((ZC, ROWS), F32), vmem((ZC, ROWS),...  126 us
    pallas_call x1, Pallas kernels, per_device(): pl.pallas_call(hand_over, out_shape=tuple((jax.ShapeDtypeStruct(out.shape...  4.37 us

profile of v5, /device:TPU:1, one launch (start us, length us, event | category | flops | bytes accessed | tf_op | source)
XLA Modules:
  0.0 131.2 jit_solution(6171191835768875038)
XLA Ops:
  0.6 126.2 %outer_step_and_projection_grads.1 = (f32[160,512]{1,0:T(8,128)S(1)}, f32[160,512]{1,0:T(8,128)S(1)}, bf16[512,5120]{1,0:T(8,128)(2,1)S(1)}, bf16[1,512,2560]{2,1,0:T(8,128)(2,1)S(1)}, bf16[1,640,2560]{2,1,0:T(8,128)(2,1)S(1)}) custom-call(bf16[1,512,5120]{2,1,0:T(8,128)(2,1)} %deltas.1, f32[160,512]{1,0:T(8,128)} %bitcast.4, f32[160,512]{1,0:T(8,128)} %bitcast.5, ...), custom_call_target="tpu_custom_call" | custom-call | flops 13421772800 | bytes 41943040 | tf_op jit(solution)/shard_map/outer_step_and_projection_grads/pallas_call | solution.py:354
  126.8 4.4 %hand_over.1 = (f32[160,512]{1,0:T(8,128)}, f32[160,512]{1,0:T(8,128)}, bf16[512,5120]{1,0:T(8,128)(2,1)}, bf16[1,512,2560]{2,1,0:T(8,128)(2,1)}, bf16[1,640,2560]{2,1,0:T(8,128)(2,1)}) custom-call(f32[160,512]{1,0:T(8,128)S(1)} %get-tuple-element.15.refs_0_, f32[160,512]{1,0:T(8,128)S(1)} %get-tuple-element.16.refs_1_, ...), custom_call_target="tpu_custom_call" | custom-call | tf_op jit(solution)/shard_map/hand_over/pallas_call | solution.py:404

commit v6 on v5

--- a/solution.py
+++ b/solution.py
@@ -15,9 +15,9 @@
 HALF = ROWS // 2
 XC, YC, ZC = D // 4, D // 16, D // 32
 TOK, DIN, DOUT, KC = 512, 2560, 2560, 640
-FIRST, SECOND = 1, 2
+FIRST, SECOND = 1, 1
 REPLICAS = 32
-N_SEMS = 31
+N_SEMS = 16
 N_LOCAL = 10
 
 
@@ -62,15 +62,17 @@
         sent.append(copy)
         return copy
 
-    def together(whole, pieces):
+    def together(whole):
         i = counts["remote"]
         counts["remote"] += 1
         sems = {"send_sem": send_sems.at[i], "recv_sem": recv_sems.at[i], "device_id_type": MESH}
-        for src, dst, device in pieces:
+
+        def send(src, dst, device):
             pltpu.make_async_remote_copy(src_ref=src, dst_ref=dst, device_id=device, **sems).start()
+
         copy = pltpu.make_async_remote_copy(src_ref=whole, dst_ref=whole, device_id=sibling, **sems)
         sent.append(copy)
-        return copy
+        return send, copy
 
     def local(src, dst):
         if free:
@@ -105,20 +107,21 @@
         tell(barrier, sibling)
         pl.semaphore_wait(chip_sem, 1)
 
-    far_c, far_i = [], []
+    send_far_c, far_c = together(c_all.at[2])
+    send_far_i, far_i = together(i_all.at[pl.ds(2, 2)])
     queue = []
-    for start, size in ((0, 480), (480, 32)):
+    for start, size in ((0, 512),):
         rows = pl.ds(start, size)
-        queue.append((far_c, cotangent.at[0, rows], c_all.at[2, rows], far))
+        queue.append((send_far_c, cotangent.at[0, rows], c_all.at[2, rows], far))
     for start, size in ((0, 256), (256, 256)):
         rows = pl.ds(start, size)
         for slot, owner, device in ((2, f_p, far), (3, f_q, diagonal)):
-            queue.append((far_i, inputs.at[0, rows, ds(owner * KC, KC)], i_all.at[slot, rows], device))
+            queue.append((send_far_i, inputs.at[0, rows, ds(owner * KC, KC)], i_all.at[slot, rows], device))
 
     def send_far(count):
         for _ in range(count):
-            kept, src, dst, device = queue.pop(0)
-            kept.append(remote(src, dst, device))
+            send, src, dst, device = queue.pop(0)
+            send(src, dst, device)
 
     send_far(FIRST)
 
@@ -143,17 +146,16 @@
     def _():
         pl.semaphore_wait(others_sem, 1)
 
-    a1_in = together(a_in.at[pl.ds(1, 3)], [
-        (deltas.at[0, pl.ds(0, HALF), ds((x + j) % 4 * XC, XC)], a_in.at[j], over_x[j - 1])
-        for j in (1, 3, 2)
-    ])
+    send, a1_in = together(a_in.at[pl.ds(1, 3)])
+    for j in (1, 3, 2):
+        send(deltas.at[0, pl.ds(0, HALF), ds((x + j) % 4 * XC, XC)], a_in.at[j], over_x[j - 1])
     load_a = local(deltas.at[0, pl.ds(0, HALF), ds(x * XC, XC)], a_in.at[0])
     load_c = local(cotangent.at[0], c_all.at[0])
     load_w = local(weight.at[0], w_all)
     load_i = local(inputs.at[0, :, ds(f * KC, KC)], i_all.at[0])
     load_m = [local(master, mast), local(momentum, mom)]
 
-    b1_sems = {"send_sem": send_sems.at[counts["remote"]], "recv_sem": recv_sems.at[counts["remote"]]}
+    send, b1_in = together(b1)
     for k in range(4):
         landed(load_b[k])
 
@@ -163,11 +165,7 @@
 
         for j in (1, 3, 2):
             there = (y + j) % 4
-            pltpu.make_async_remote_copy(
-                src_ref=b_t.at[k, ds(there * YC, YC)], dst_ref=b1.at[j - 1, k],
-                device_id=over_y[j - 1], device_id_type=MESH, **b1_sems,
-            ).start()
-    b1_in = together(b1, [])
+            send(b_t.at[k, ds(there * YC, YC)], b1.at[j - 1, k], over_y[j - 1])
 
     near_c = remote(cotangent.at[0], c_all.at[1], sibling)
     near_i = remote(inputs.at[0, :, ds(f_s * KC, KC)], i_all.at[1], sibling)
@@ -193,7 +191,8 @@
     store(d_all.at[0], o_input_grad.at[0, :, mine])
     near_c.wait_recv()
     grad_of(1)
-    grads = [remote(d_all.at[1], o_input_grad.at[0, :, mine], sibling)]
+    send_grad, grads = together(d_all.at[pl.ds(1, 3)])
+    send_grad(d_all.at[1], o_input_grad.at[0, :, mine], sibling)
     landed(load_i)
     turn(0)
     near_i.wait_recv()
@@ -210,9 +209,9 @@
             total += a_in[j, :, columns].astype(F32)
         a_t[columns, :] = total.astype(BF16).T
 
-    a2_in = together(a2, [
-        (a_t.at[ds((y + j) % 4 * YC, YC)], a2.at[j - 1], over_y[j - 1]) for j in (1, 3, 2)
-    ])
+    send, a2_in = together(a2)
+    for j in (1, 3, 2):
+        send(a_t.at[ds((y + j) % 4 * YC, YC)], a2.at[j - 1], over_y[j - 1])
     b1_in.wait_recv()
 
     @pl.loop(0, 4)
@@ -225,7 +224,9 @@
                 total += b1[j, k, rows, :].astype(F32)
             v_b[k, rows, :] = total.astype(BF16)
 
-    b2_in = together(b2, [(v_b.at[(x + j) % 4], b2.at[j - 1], over_x[j - 1]) for j in (1, 3, 2)])
+    send, b2_in = together(b2)
+    for j in (1, 3, 2):
+        send(v_b.at[(x + j) % 4], b2.at[j - 1], over_x[j - 1])
 
     a2_in.wait_recv()
     b2_in.wait_recv()
@@ -265,11 +266,12 @@
     store(mom, o_momentum)
     n_in.wait_recv()
 
-    second = []
     here = ds(y * YC, YC)
-    for j in (1, 3, 2):
-        second.append(remote(new.at[:, pl.ds(0, HALF)], new_a.at[here], over_y[j - 1]))
-        second.append(remote(new.at[:, pl.ds(HALF, HALF)], new_b.at[x, here], over_x[j - 1]))
+    send_a, a2_out = together(a2)
+    send_b, b2_out = together(b2)
+    for j in (1, 3, 2):
+        send_a(new.at[:, pl.ds(0, HALF)], new_a.at[here], over_y[j - 1])
+        send_b(new.at[:, pl.ds(HALF, HALF)], new_b.at[x, here], over_x[j - 1])
 
     @pl.loop(0, YC // 32)
     def _(n):
@@ -277,37 +279,32 @@
         new_a[ds(y * YC + n * 32, 32), :] = new[rows, pl.ds(0, HALF)]
         new_b[x, ds(y * YC + n * 32, 32), :] = new[rows, pl.ds(HALF, HALF)]
 
-    forwards = []
-    for copy, rows in zip(far_c, (pl.ds(0, 480), pl.ds(480, 32))):
-        copy.wait_recv()
-        forwards.append(remote(c_all.at[2, rows], c_all.at[3, rows], sibling))
-    for copy in second:
-        copy.wait_recv()
-    first = []
-    for j in (1, 3, 2):
-        first.append(remote(new_b.at[:, here], new_b.at[:, here], over_y[j - 1]))
+    far_c.wait_recv()
+    forward = remote(c_all.at[2], c_all.at[3], sibling)
+    a2_out.wait_recv()
+    b2_out.wait_recv()
+    send, b1_out = together(b1)
+    for j in (1, 3, 2):
+        send(new_b.at[:, here], new_b.at[:, here], over_y[j - 1])
 
     @pl.loop(0, XC // 128)
     def _(n):
         new_ar[:, ds(n * 128, 128)] = new_a[ds(n * 128, 128), :].T
 
     theirs = o_weights.at[pl.ds(0, HALF), ds(x * XC, XC)]
-    for j in (1, 3, 2):
-        first.append(remote(new_ar, theirs, over_x[j - 1]))
+    send, a1_out = together(a_in.at[pl.ds(1, 3)])
+    for j in (1, 3, 2):
+        send(new_ar, theirs, over_x[j - 1])
     store(new_ar, theirs)
 
     grad_of(2)
-    grads.append(remote(d_all.at[2], o_input_grad.at[0, :, mine], far))
-    for copy in forwards:
-        copy.wait_recv()
+    send_grad(d_all.at[2], o_input_grad.at[0, :, mine], far)
+    forward.wait_recv()
     grad_of(3)
-    grads.append(remote(d_all.at[3], o_input_grad.at[0, :, mine], diagonal))
-
-    for copy in far_i[0::2]:
-        copy.wait_recv()
+    send_grad(d_all.at[3], o_input_grad.at[0, :, mine], diagonal)
+
+    far_i.wait_recv()
     turn(2)
-    for copy in far_i[1::2]:
-        copy.wait_recv()
     turn(3)
 
     @pl.loop(0, DOUT // 256)
@@ -320,8 +317,8 @@
 
     store(g_all, o_weight_grad.at[0])
 
-    for copy in first:
-        copy.wait_recv()
+    b1_out.wait_recv()
+    a1_out.wait_recv()
     for k in range(4):
         @pl.loop(0, XC // 256)
         def _(n):
@@ -330,14 +327,12 @@
         columns = pl.ds(XC * k, XC)
         store(b_in.at[:, columns], o_weights.at[pl.ds(HALF, HALF), columns])
 
-    for copy in sent[:-2]:
-        copy.wait_send()
+    for copy in sent:
+        if copy is not grads:
+            copy.wait_send()
     for copy in stored:
         copy.wait()
-    for copy in grads:
-        copy.wait_recv()
-    for copy in sent[-2:]:
-        copy.wait_send()
+    grads.wait()
 
 
 def hand_over(*refs):

time: 131 us -> 131 us (level)
  no operation moved by 1% of the time
where the time goes in v6:
time: 131 us
  Pallas kernels  130 us (99%)
    pallas_call x1, Pallas kernels, per_device(): pl.pallas_call(kernel, out_shape=(vmem((ZC, ROWS), F32), vmem((ZC, ROWS),...  126 us
    pallas_call x1, Pallas kernels, per_device(): pl.pallas_call(hand_over, out_shape=tuple((jax.ShapeDtypeStruct(out.shape...  4.37 us

profile of v6, /device:TPU:1, one launch (start us, length us, event | category | flops | bytes accessed | tf_op | source)
XLA Modules:
  0.0 130.9 jit_solution(3722667457033219631)
XLA Ops:
  0.6 125.9 %outer_step_and_projection_grads.1 = (f32[160,512]{1,0:T(8,128)S(1)}, f32[160,512]{1,0:T(8,128)S(1)}, bf16[512,5120]{1,0:T(8,128)(2,1)S(1)}, bf16[1,512,2560]{2,1,0:T(8,128)(2,1)S(1)}, bf16[1,640,2560]{2,1,0:T(8,128)(2,1)S(1)}) custom-call(bf16[1,512,5120]{2,1,0:T(8,128)(2,1)} %deltas.1, f32[160,512]{1,0:T(8,128)} %bitcast.4, f32[160,512]{1,0:T(8,128)} %bitcast.5, ...), custom_call_target="tpu_custom_call" | custom-call | flops 13421772800 | bytes 41943040 | tf_op jit(solution)/shard_map/outer_step_and_projection_grads/pallas_call | solution.py:349
  126.5 4.4 %hand_over.1 = (f32[160,512]{1,0:T(8,128)}, f32[160,512]{1,0:T(8,128)}, bf16[512,5120]{1,0:T(8,128)(2,1)}, bf16[1,512,2560]{2,1,0:T(8,128)(2,1)}, bf16[1,640,2560]{2,1,0:T(8,128)(2,1)}) custom-call(f32[160,512]{1,0:T(8,128)S(1)} %get-tuple-element.15.refs_0_, f32[160,512]{1,0:T(8,128)S(1)} %get-tuple-element.16.refs_1_, ...), custom_call_target="tpu_custom_call" | custom-call | tf_op jit(solution)/shard_map/hand_over/pallas_call | solution.py:399

commit v7 on v6

--- a/solution.py
+++ b/solution.py
@@ -17,7 +17,7 @@
 TOK, DIN, DOUT, KC = 512, 2560, 2560, 640
 FIRST, SECOND = 1, 1
 REPLICAS = 32
-N_SEMS = 16
+N_SEMS = 14
 N_LOCAL = 10
 
 
@@ -113,10 +113,11 @@
     for start, size in ((0, 512),):
         rows = pl.ds(start, size)
         queue.append((send_far_c, cotangent.at[0, rows], c_all.at[2, rows], far))
-    for start, size in ((0, 256), (256, 256)):
+    for slot, owner, device, start, size in (
+        (2, f_p, far, 0, 256), (2, f_p, far, 256, 256), (3, f_q, diagonal, 0, TOK)
+    ):
         rows = pl.ds(start, size)
-        for slot, owner, device in ((2, f_p, far), (3, f_q, diagonal)):
-            queue.append((send_far_i, inputs.at[0, rows, ds(owner * KC, KC)], i_all.at[slot, rows], device))
+        queue.append((send_far_i, inputs.at[0, rows, ds(owner * KC, KC)], i_all.at[slot, rows], device))
 
     def send_far(count):
         for _ in range(count):
@@ -209,9 +210,10 @@
             total += a_in[j, :, columns].astype(F32)
         a_t[columns, :] = total.astype(BF16).T
 
-    send, a2_in = together(a2)
-    for j in (1, 3, 2):
-        send(a_t.at[ds((y + j) % 4 * YC, YC)], a2.at[j - 1], over_y[j - 1])
+    both = b1.at[pl.ds(0, 2), pl.ds(0, 3)]
+    send_second, second_in = together(both)
+    for j in (1, 3, 2):
+        send_second(a_t.at[ds((y + j) % 4 * YC, YC)], a2.at[j - 1], over_y[j - 1])
     b1_in.wait_recv()
 
     @pl.loop(0, 4)
@@ -224,12 +226,10 @@
                 total += b1[j, k, rows, :].astype(F32)
             v_b[k, rows, :] = total.astype(BF16)
 
-    send, b2_in = together(b2)
-    for j in (1, 3, 2):
-        send(v_b.at[(x + j) % 4], b2.at[j - 1], over_x[j - 1])
-
-    a2_in.wait_recv()
-    b2_in.wait_recv()
+    for j in (1, 3, 2):
+        send_second(v_b.at[(x + j) % 4], b2.at[j - 1], over_x[j - 1])
+
+    second_in.wait_recv()
 
     @pl.loop(0, YC // 32)
     def _(n):
@@ -267,11 +267,10 @@
     n_in.wait_recv()
 
     here = ds(y * YC, YC)
-    send_a, a2_out = together(a2)
-    send_b, b2_out = together(b2)
-    for j in (1, 3, 2):
-        send_a(new.at[:, pl.ds(0, HALF)], new_a.at[here], over_y[j - 1])
-        send_b(new.at[:, pl.ds(HALF, HALF)], new_b.at[x, here], over_x[j - 1])
+    send, second_out = together(both)
+    for j in (1, 3, 2):
+        send(new.at[:, pl.ds(0, HALF)], new_a.at[here], over_y[j - 1])
+        send(new.at[:, pl.ds(HALF, HALF)], new_b.at[x, here], over_x[j - 1])
 
     @pl.loop(0, YC // 32)
     def _(n):
@@ -281,8 +280,7 @@
 
     far_c.wait_recv()
     forward = remote(c_all.at[2], c_all.at[3], sibling)
-    a2_out.wait_recv()
-    b2_out.wait_recv()
+    second_out.wait_recv()
     send, b1_out = together(b1)
     for j in (1, 3, 2):
         send(new_b.at[:, here], new_b.at[:, here], over_y[j - 1])

time: 131 us -> 131 us (level)
  no operation moved by 1% of the time
where the time goes in v7:
time: 131 us
  Pallas kernels  130 us (99%)
    pallas_call x1, Pallas kernels, per_device(): pl.pallas_call(kernel, out_shape=(vmem((ZC, ROWS), F32), vmem((ZC, ROWS),...  126 us
    pallas_call x1, Pallas kernels, per_device(): pl.pallas_call(hand_over, out_shape=tuple((jax.ShapeDtypeStruct(out.shape...  4.37 us

profile of v7, /device:TPU:1, one launch (start us, length us, event | category | flops | bytes accessed | tf_op | source)
XLA Modules:
  0.0 130.9 jit_solution(1931937981127839322)
XLA Ops:
  0.6 125.9 %outer_step_and_projection_grads.1 = (f32[160,512]{1,0:T(8,128)S(1)}, f32[160,512]{1,0:T(8,128)S(1)}, bf16[512,5120]{1,0:T(8,128)(2,1)S(1)}, bf16[1,512,2560]{2,1,0:T(8,128)(2,1)S(1)}, bf16[1,640,2560]{2,1,0:T(8,128)(2,1)S(1)}) custom-call(bf16[1,512,5120]{2,1,0:T(8,128)(2,1)} %deltas.1, f32[160,512]{1,0:T(8,128)} %bitcast.4, f32[160,512]{1,0:T(8,128)} %bitcast.5, ...), custom_call_target="tpu_custom_call" | custom-call | flops 13421772800 | bytes 41943040 | tf_op jit(solution)/shard_map/outer_step_and_projection_grads/pallas_call | solution.py:347
  126.5 4.4 %hand_over.1 = (f32[160,512]{1,0:T(8,128)}, f32[160,512]{1,0:T(8,128)}, bf16[512,5120]{1,0:T(8,128)(2,1)}, bf16[1,512,2560]{2,1,0:T(8,128)(2,1)}, bf16[1,640,2560]{2,1,0:T(8,128)(2,1)}) custom-call(f32[160,512]{1,0:T(8,128)S(1)} %get-tuple-element.15.refs_0_, f32[160,512]{1,0:T(8,128)S(1)} %get-tuple-element.16.refs_1_, ...), custom_call_target="tpu_custom_call" | custom-call | tf_op jit(solution)/shard_map/hand_over/pallas_call | solution.py:397
